TPU v7x, 512 devices: a whole 4x8x8 slice. The times are simulated.
512 devices in a mesh: loop: 16 (over y, x_hi), dp: 32 (over z, x_lo, core).
Axes of the slice: x: 4 (x_hi: 2, x_lo: 2; x = x_hi * 2 + x_lo), y: 8, z: 8, core: 2. Of those that a mesh axis runs over, the one named last changes fastest.
Arguments:
- images: bfloat16 [32, 32, 16, 16, 768], P('dp', 'loop'), may hold values from -6 to 6
- kernel: float32 [7, 7, 768], replicated, may hold values from -0.875 to 0.875
- ln_gain: float32 [768], replicated, may hold values from 0.5 to 1.5
- w_up: bfloat16 [768, 1536], P('dp'), may hold values from -0.21875 to 0.21875
- b_up: float32 [1536], replicated, may hold values from -3 to 3
- w_down: bfloat16 [1536, 768], P('dp'), may hold values from -0.15625 to 0.15625
- layer_scale: float32 [768], replicated, may hold values from 0.3 to 1
- w_head: bfloat16 [768, 1152], P('dp'), may hold values from -0.21875 to 0.21875
- text_rows: bfloat16 [32, 32, 1152], P('dp', 'loop'), may hold values from -6 to 6
- pair_ids: int32 [32, 32], P('dp', 'loop'), may hold values from 0 to 31, each once within a row
- log_temp: float32 [1], replicated, may hold values from 1.5 to 2.5
- loss_bias: float32 [1], replicated, may hold values from -6 to -2
Outputs:
- kernel_grad: float32 [7, 7, 768], replicated
- up_grad: float32 [768, 1536], P('dp')
- text_grad: float32 [32, 32, 1152], P('dp', 'loop')
Inputs may be any that keep to these rules, and one draw needn't show every extreme that they name: Each row of pair_ids holds every index of its group once.
All inputs are finite; a program needn't handle non-finite values.
Results may differ from a plain program's by a relative error of at most 0.04.
Values may be sent and summed in bfloat16 or wider, within the bound.
A program may use at most 64 MiB of HBM per device.

v0:
```python
import jax
import jax.numpy as jnp
from jax import lax
from jax.sharding import PartitionSpec as P

epsilon = 1e-06


def passed_along(value, axis, steps):
    count = lax.axis_size(axis)
    pairs = [(source, (source + steps) % count) for source in range(count)]
    return lax.ppermute(value, axis, pairs)


def image_tower(kernel, w_up, images, ln_gain, b_up, w_down, layer_scale, w_head):
    image_count = images.shape[0]
    grid_side = images.shape[1]
    channels = images.shape[3]
    padded = jnp.pad(images, ((0, 0), (3, 3), (3, 3), (0, 0)))
    conv_out = jnp.zeros(images.shape, jnp.float32)
    for row_off in range(7):
        for col_off in range(7):
            window = padded[:, row_off : row_off + grid_side, col_off : col_off + grid_side, :]
            conv_out = conv_out + window.astype(jnp.float32) * kernel[row_off, col_off]
    chan_mean = jnp.mean(conv_out, axis=-1, keepdims=True)
    centered = conv_out - chan_mean
    chan_var = jnp.mean(centered * centered, axis=-1, keepdims=True)
    normed = (centered * lax.rsqrt(chan_var + epsilon) * ln_gain).astype(jnp.bfloat16)
    flat_rows = normed.reshape(-1, channels)
    hidden = jnp.dot(flat_rows, w_up, preferred_element_type=jnp.float32) + b_up
    active = jax.nn.gelu(hidden, approximate=True).astype(jnp.bfloat16)
    mlp_out = jnp.dot(active, w_down, preferred_element_type=jnp.float32)
    block_out = images.reshape(-1, channels).astype(jnp.float32) + layer_scale * mlp_out
    pooled = jnp.mean(
        block_out.reshape(image_count, grid_side * grid_side, channels), axis=1
    ).astype(jnp.bfloat16)
    embedding = jnp.dot(pooled, w_head, preferred_element_type=jnp.float32)
    return embedding * lax.rsqrt(jnp.sum(embedding * embedding, axis=-1, keepdims=True) + epsilon)


def pair_grad(image_emb, text_emb, pair_row, text_index, logit_scale, logit_bias, group_size):
    logits = (
        logit_scale * jnp.dot(image_emb, text_emb.T, precision=lax.Precision.HIGHEST) + logit_bias
    )
    sign_of = jnp.where(pair_row[:, None] == text_index[None, :], 1.0, -1.0)
    return -sign_of * jax.nn.sigmoid(-sign_of * logits) / group_size


def body(
    images,
    kernel,
    ln_gain,
    w_up,
    b_up,
    w_down,
    layer_scale,
    w_head,
    text_rows,
    pair_ids,
    log_temp,
    loss_bias,
):
    loop_size = lax.axis_size("loop")
    loop_index = lax.axis_index("loop")
    up_full, down_full, head_full = (
        lax.all_gather(w_up, "dp", axis=0, tiled=True),
        lax.all_gather(w_down, "dp", axis=0, tiled=True),
        lax.all_gather(w_head, "dp", axis=0, tiled=True),
    )
    pictures = images[0]
    pair_row = pair_ids[0]
    img_dev = pictures.shape[0]
    group_size = img_dev * loop_size
    logit_scale = jnp.exp(log_temp[0])
    logit_bias = loss_bias[0]

    def run_tower(kernel_arg, up_arg):
        return image_tower(
            kernel_arg, up_arg, pictures, ln_gain, b_up, down_full, layer_scale, head_full
        )

    image_emb, pullback = jax.vjp(run_tower, kernel, up_full)
    raw_rows = text_rows[0].astype(jnp.float32)
    text_norm = jnp.sqrt(jnp.sum(raw_rows * raw_rows, axis=-1, keepdims=True) + epsilon)
    text_hat = raw_rows / text_norm
    rounded = lax.optimization_barrier(text_hat.astype(jnp.bfloat16))
    local_index = jnp.arange(img_dev, dtype=jnp.int32)

    def cycle_step(step_index, state):
        text_block, partials, image_cot = state
        source = (loop_index - step_index) % loop_size
        text_index = source * img_dev + local_index
        pair_weight = pair_grad(
            image_emb, text_block, pair_row, text_index, logit_scale, logit_bias, group_size
        )
        image_cot = image_cot + logit_scale * jnp.dot(
            pair_weight, text_block, precision=lax.Precision.HIGHEST
        )
        partials = partials + logit_scale * jnp.dot(
            pair_weight.T, image_emb, precision=lax.Precision.HIGHEST
        )
        text_block, partials = passed_along((text_block, partials), "loop", 1)
        return (text_block, partials, image_cot)

    start = (
        rounded.astype(jnp.float32),
        jnp.zeros(raw_rows.shape, jnp.float32),
        jnp.zeros(image_emb.shape, jnp.float32),
    )
    _, text_cot, image_cot = lax.fori_loop(0, loop_size, cycle_step, start)
    text_grad = (
        text_cot - text_hat * jnp.sum(text_hat * text_cot, axis=-1, keepdims=True)
    ) / text_norm
    kernel_part, up_part = pullback(image_cot)
    kernel_grad = lax.psum(kernel_part, ("loop", "dp"))
    up_rows = lax.psum_scatter(
        up_part.astype(jnp.float32).astype(jnp.bfloat16), "dp", scatter_dimension=0, tiled=True
    )
    up_grad = lax.psum(up_rows, "loop").astype(jnp.float32)
    return (kernel_grad, up_grad, text_grad[None])


def solution(mesh):
    placed = (
        P("dp", "loop", None, None, None),
        P(),
        P(),
        P("dp", None),
        P(),
        P("dp", None),
        P(),
        P("dp", None),
        P("dp", "loop", None),
        P("dp", "loop"),
        P(),
        P(),
    )
    return jax.shard_map(
        body,
        mesh=mesh,
        in_specs=placed,
        out_specs=(P(), P("dp", None), P("dp", "loop", None)),
        check_vma=False,
    )
```

profile of v0, /device:TPU:1, one launch (start us, length us, event | category | flops | bytes accessed | tf_op | source)
XLA Modules:
  0.0 996.5 jit_solution(3485320233537033907)
XLA Ops:
  15.5 30.5 %fusion.140 = (f32[2,16,16]{2,1,0:T(8,128)S(1)}, f32[2,16,16,768]{3,2,1,0:T(8,128)S(1)}) fusion(f32[768]{0:T(1024)S(1)} %get-tuple-element.377, f32[768]{0:T(1024)S(1)} %get-tuple-element.378, f32[768]{0:T(1024)S(1)} %get-tuple-element.331, f32[768]{0:T(1024)S(1)} %get-tuple-element.332, f32[768]{0:T(1024)S(1)} %get-tuple-element.333, ...), kind=kLoop, calls=%fused_computation.374 | loop fusion | flops 57802240 | bytes 2511872 | tf_op jit(solution)/shard_map/jvp()/reduce_sum | solution.py:25
  46.7 37.7 %all-gather.4.cloned.1.call-done = bf16[768,1536]{1,0:T(8,128)(2,1)} async-done(((bf16[24,1536]{1,0:T(8,128)(2,1)}), bf16[768,1536]{1,0:T(8,128)(2,1)}) %all-gather.4.cloned.1.call-update) | async-done | bytes 2359312 | tf_op jit(solution)/shard_map/all_gather | solution.py:66
  84.4 4.8 convolution_add_fusion
  89.2 65.1 %all-gather.6.cloned.1.call-done = bf16[1536,768]{1,0:T(8,128)(2,1)} async-done(((bf16[48,768]{1,0:T(8,128)(2,1)}), bf16[1536,768]{1,0:T(8,128)(2,1)}) %all-gather.6.cloned.1.call-update) | async-done | bytes 2359312 | tf_op jit(solution)/shard_map/all_gather | solution.py:67
  154.3 4.6 bitcast_reduce_fusion
  158.9 64.5 %all-gather.8.cloned.1.call-done = bf16[768,1152]{1,0:T(8,128)(2,1)} async-done(((bf16[24,1152]{1,0:T(8,128)(2,1)}), bf16[768,1152]{1,0:T(8,128)(2,1)}) %all-gather.8.cloned.1.call-update) | async-done | bytes 1769488 | tf_op jit(solution)/shard_map/all_gather | solution.py:68
  225.4 184.7 %while.20 = (s32[]{:T(128)}, f32[2,1152]{1,0:T(2,128)S(1)}, f32[2,1152]{1,0:T(2,128)S(1)}, f32[2,1152]{1,0:T(2,128)S(1)}, f32[]{:T(128)}, /*index=5*/s32[1,2]{1,...) while((s32[]{:T(128)}, f32[2,1152]{1,0:T(2,128)S(1)}, ...), condition=%wide.region_6.7_spmd.clone, body=%wide.region_5.6_spmd.clone.sunk | while | flops 177470 | bytes 166336 | solution.py:110
  225.5 4.3 collective-permute-start
  230.9 3.4 collective-permute-start.1
  234.5 4.4 collective-permute-done.1
  242.0 4.6 collective-permute-start.1
  246.8 3.2 collective-permute-done.1
  253.7 3.4 collective-permute-start.1
  257.3 4.4 collective-permute-done.1
  264.8 4.6 collective-permute-start.1
  269.5 3.2 collective-permute-done.1
  276.4 3.4 collective-permute-start.1
  280.0 4.4 collective-permute-done.1
  287.5 4.6 collective-permute-start.1
  292.3 3.2 collective-permute-done.1
  299.1 5.2 collective-permute-start.1
  307.1 3.1 collective-permute-start
  311.4 6.0 collective-permute-start.1
  319.4 3.9 collective-permute-start
  324.4 3.9 collective-permute-start.1
  328.5 4.0 collective-permute-done.1
  335.6 3.8 collective-permute-start.1
  339.6 4.1 collective-permute-done.1
  346.7 3.8 collective-permute-start.1
  350.7 4.1 collective-permute-done.1
  357.8 3.8 collective-permute-start.1
  361.8 4.1 collective-permute-done.1
  368.9 3.8 collective-permute-start.1
  372.8 4.1 collective-permute-done.1
  380.0 3.8 collective-permute-start.1
  384.0 4.0 collective-permute-done.1
  391.1 3.8 collective-permute-start.1
  395.0 4.1 collective-permute-done.1
  402.2 4.1 collective-permute-start.1
  406.5 3.7 collective-permute-done.1
  412.6 4.6 fusion.14
  421.3 3.6 fusion.143
  426.0 5.0 fusion.117
  431.1 3.7 fusion.23
  434.9 3.9 fusion.118
  440.1 119.1 %reduce-scatter.2.cloned.1.call-done = bf16[24,1536]{1,0:T(8,128)(2,1)} async-done(((bf16[768,1536]{1,0:T(8,128)(2,1)}), bf16[24,1536]{1,0:T(8,128)(2,1)}) %reduce-scatter.2.cloned.1.call-update) | async-done | bytes 73744 | tf_op jit(solution)/shard_map/reduce_scatter | solution.py:116
  560.5 148.9 %all-reduce.55.cloned.1.call-done = bf16[24,1536]{1,0:T(8,128)(2,1)} async-done(((bf16[24,1536]{1,0:T(8,128)(2,1)}), bf16[24,1536]{1,0:T(8,128)(2,1)}) %all-reduce.55.cloned.1.call-update) | async-done | bytes 73744 | tf_op jit(solution)/shard_map/psum | solution.py:119
  711.0 277.1 %all-reduce.53.cloned.1.call-done = f32[7,7,768]{2,1,0:T(8,128)} async-done(((f32[7,7,768]{2,1,0:T(8,128)}), f32[7,7,768]{2,1,0:T(8,128)}) %all-reduce.53.cloned.1.call-update) | async-done | bytes 150544 | tf_op jit(solution)/shard_map/psum | solution.py:115
  (216 shorter events, 74.9 us)
Async XLA Ops:
  7.2 77.2 %all-gather.4.cloned.1.call-start = ((), (), s32[]{:S(2)}) async-start(), calls=%async_computation.1 | async-start | bytes 2433024 | tf_op jit(solution)/shard_map/all_gather | solution.py:66
  7.9 146.4 %all-gather.6.cloned.1.call-start = ((), (), s32[]{:S(2)}) async-start(), calls=%async_computation.2 | async-start | bytes 2433024 | tf_op jit(solution)/shard_map/all_gather | solution.py:67
  8.6 214.8 %all-gather.8.cloned.1.call-start = ((), (), s32[]{:S(2)}) async-start(), calls=%async_computation.3 | async-start | bytes 1824768 | tf_op jit(solution)/shard_map/all_gather | solution.py:68
  9.4 549.9 %reduce-scatter.2.cloned.1.call-start = ((), (), s32[]{:S(2)}) async-start(), calls=%async_computation.5 | async-start | bytes 2433024 | tf_op jit(solution)/shard_map/reduce_scatter | solution.py:116
  15.5 30.9 %copy-start.1 = (f32[768]{0:T(1024)S(1)}, f32[768]{0:T(1024)}, u32[]{:S(2)}) copy-start(f32[768]{0:T(1024)} %param.16) | copy-start | bytes 9220
  46.4 38.0 %copy-start.4 = (f32[1536]{0:T(1024)S(1)}, f32[1536]{0:T(1024)}, u32[]{:S(2)}) copy-start(f32[1536]{0:T(1024)} %param.18) | copy-start | bytes 18436
  84.4 69.9 %copy-start = (bf16[1,2,16,16,768]{4,3,2,1,0:T(8,128)(2,1)S(1)}, bf16[1,2,16,16,768]{4,3,2,1,0:T(8,128)(2,1)}, u32[]{:S(2)}) copy-start(bf16[1,2,16,16,768]{4,3,2,1,0:T(8,128)(2,1)} %param.14) | copy-start | bytes 2359300
  84.4 69.9 %copy-start.2 = (f32[768]{0:T(1024)S(1)}, f32[768]{0:T(1024)}, u32[]{:S(2)}) copy-start(f32[768]{0:T(1024)} %param.20) | copy-start | bytes 9220
  158.9 66.5 %copy-start.5 = (s32[1,2]{1,0:T(1,128)S(1)}, s32[1,2]{1,0:T(1,128)}, u32[]{:S(2)}) copy-start(s32[1,2]{1,0:T(1,128)} %param.23) | copy-start | bytes 28
  225.5 13.5 %collective-permute-start = (f32[2,1152]{1,0:T(2,128)S(1)}, f32[2,1152]{1,0:T(2,128)S(1)}, u32[]{:S(2)}, u32[]{:S(2)}) collective-permute-start(f32[2,1152]{1,0:T(2,128)S(1)} %copy.20), channel_id=1, source_target_pairs={{0,32},{32,64},{64,96},{96,128},{128,160},{160,192},{192,224},{224... | collective-permute-start | bytes 27656 | tf_op jit(solution)/shard_map/while/body/eval_jaxpr/ppermute | solution.py:12
  230.9 8.0 collective-permute-start.1
  239.0 11.1 %collective-permute-start = (f32[2,1152]{1,0:T(2,128)S(1)}, f32[2,1152]{1,0:T(2,128)S(1)}, u32[]{:S(2)}, u32[]{:S(2)}) collective-permute-start(f32[2,1152]{1,0:T(2,128)S(1)} %copy.20), channel_id=1, source_target_pairs={{0,32},{32,64},{64,96},{96,128},{128,160},{160,192},{192,224},{224... | collective-permute-start | bytes 27656 | tf_op jit(solution)/shard_map/while/body/eval_jaxpr/ppermute | solution.py:12
  242.0 8.0 collective-permute-start.1
  250.1 11.6 %collective-permute-start = (f32[2,1152]{1,0:T(2,128)S(1)}, f32[2,1152]{1,0:T(2,128)S(1)}, u32[]{:S(2)}, u32[]{:S(2)}) collective-permute-start(f32[2,1152]{1,0:T(2,128)S(1)} %copy.20), channel_id=1, source_target_pairs={{0,32},{32,64},{64,96},{96,128},{128,160},{160,192},{192,224},{224... | collective-permute-start | bytes 27656 | tf_op jit(solution)/shard_map/while/body/eval_jaxpr/ppermute | solution.py:12
  253.7 8.0 collective-permute-start.1
  261.7 11.1 %collective-permute-start = (f32[2,1152]{1,0:T(2,128)S(1)}, f32[2,1152]{1,0:T(2,128)S(1)}, u32[]{:S(2)}, u32[]{:S(2)}) collective-permute-start(f32[2,1152]{1,0:T(2,128)S(1)} %copy.20), channel_id=1, source_target_pairs={{0,32},{32,64},{64,96},{96,128},{128,160},{160,192},{192,224},{224... | collective-permute-start | bytes 27656 | tf_op jit(solution)/shard_map/while/body/eval_jaxpr/ppermute | solution.py:12
  264.8 8.0 collective-permute-start.1
  272.8 11.6 %collective-permute-start = (f32[2,1152]{1,0:T(2,128)S(1)}, f32[2,1152]{1,0:T(2,128)S(1)}, u32[]{:S(2)}, u32[]{:S(2)}) collective-permute-start(f32[2,1152]{1,0:T(2,128)S(1)} %copy.20), channel_id=1, source_target_pairs={{0,32},{32,64},{64,96},{96,128},{128,160},{160,192},{192,224},{224... | collective-permute-start | bytes 27656 | tf_op jit(solution)/shard_map/while/body/eval_jaxpr/ppermute | solution.py:12
  276.4 8.0 collective-permute-start.1
  284.4 11.1 %collective-permute-start = (f32[2,1152]{1,0:T(2,128)S(1)}, f32[2,1152]{1,0:T(2,128)S(1)}, u32[]{:S(2)}, u32[]{:S(2)}) collective-permute-start(f32[2,1152]{1,0:T(2,128)S(1)} %copy.20), channel_id=1, source_target_pairs={{0,32},{32,64},{64,96},{96,128},{128,160},{160,192},{192,224},{224... | collective-permute-start | bytes 27656 | tf_op jit(solution)/shard_map/while/body/eval_jaxpr/ppermute | solution.py:12
  287.5 8.0 collective-permute-start.1
  295.5 11.6 %collective-permute-start = (f32[2,1152]{1,0:T(2,128)S(1)}, f32[2,1152]{1,0:T(2,128)S(1)}, u32[]{:S(2)}, u32[]{:S(2)}) collective-permute-start(f32[2,1152]{1,0:T(2,128)S(1)} %copy.20), channel_id=1, source_target_pairs={{0,32},{32,64},{64,96},{96,128},{128,160},{160,192},{192,224},{224... | collective-permute-start | bytes 27656 | tf_op jit(solution)/shard_map/while/body/eval_jaxpr/ppermute | solution.py:12
  299.1 8.0 collective-permute-start.1
  307.1 12.3 %collective-permute-start = (f32[2,1152]{1,0:T(2,128)S(1)}, f32[2,1152]{1,0:T(2,128)S(1)}, u32[]{:S(2)}, u32[]{:S(2)}) collective-permute-start(f32[2,1152]{1,0:T(2,128)S(1)} %copy.20), channel_id=1, source_target_pairs={{0,32},{32,64},{64,96},{96,128},{128,160},{160,192},{192,224},{224... | collective-permute-start | bytes 27656 | tf_op jit(solution)/shard_map/while/body/eval_jaxpr/ppermute | solution.py:12
  311.4 8.0 collective-permute-start.1
  319.4 13.1 %collective-permute-start = (f32[2,1152]{1,0:T(2,128)S(1)}, f32[2,1152]{1,0:T(2,128)S(1)}, u32[]{:S(2)}, u32[]{:S(2)}) collective-permute-start(f32[2,1152]{1,0:T(2,128)S(1)} %copy.20), channel_id=1, source_target_pairs={{0,32},{32,64},{64,96},{96,128},{128,160},{160,192},{192,224},{224... | collective-permute-start | bytes 27656 | tf_op jit(solution)/shard_map/while/body/eval_jaxpr/ppermute | solution.py:12
  324.4 8.0 collective-permute-start.1
  332.5 11.2 %collective-permute-start = (f32[2,1152]{1,0:T(2,128)S(1)}, f32[2,1152]{1,0:T(2,128)S(1)}, u32[]{:S(2)}, u32[]{:S(2)}) collective-permute-start(f32[2,1152]{1,0:T(2,128)S(1)} %copy.20), channel_id=1, source_target_pairs={{0,32},{32,64},{64,96},{96,128},{128,160},{160,192},{192,224},{224... | collective-permute-start | bytes 27656 | tf_op jit(solution)/shard_map/while/body/eval_jaxpr/ppermute | solution.py:12
  335.6 8.0 collective-permute-start.1
  343.7 11.1 %collective-permute-start = (f32[2,1152]{1,0:T(2,128)S(1)}, f32[2,1152]{1,0:T(2,128)S(1)}, u32[]{:S(2)}, u32[]{:S(2)}) collective-permute-start(f32[2,1152]{1,0:T(2,128)S(1)} %copy.20), channel_id=1, source_target_pairs={{0,32},{32,64},{64,96},{96,128},{128,160},{160,192},{192,224},{224... | collective-permute-start | bytes 27656 | tf_op jit(solution)/shard_map/while/body/eval_jaxpr/ppermute | solution.py:12
  346.7 8.0 collective-permute-start.1
  354.7 11.1 %collective-permute-start = (f32[2,1152]{1,0:T(2,128)S(1)}, f32[2,1152]{1,0:T(2,128)S(1)}, u32[]{:S(2)}, u32[]{:S(2)}) collective-permute-start(f32[2,1152]{1,0:T(2,128)S(1)} %copy.20), channel_id=1, source_target_pairs={{0,32},{32,64},{64,96},{96,128},{128,160},{160,192},{192,224},{224... | collective-permute-start | bytes 27656 | tf_op jit(solution)/shard_map/while/body/eval_jaxpr/ppermute | solution.py:12
  357.8 8.0 collective-permute-start.1
  365.8 11.1 %collective-permute-start = (f32[2,1152]{1,0:T(2,128)S(1)}, f32[2,1152]{1,0:T(2,128)S(1)}, u32[]{:S(2)}, u32[]{:S(2)}) collective-permute-start(f32[2,1152]{1,0:T(2,128)S(1)} %copy.20), channel_id=1, source_target_pairs={{0,32},{32,64},{64,96},{96,128},{128,160},{160,192},{192,224},{224... | collective-permute-start | bytes 27656 | tf_op jit(solution)/shard_map/while/body/eval_jaxpr/ppermute | solution.py:12
  368.9 8.0 collective-permute-start.1
  376.9 11.1 %collective-permute-start = (f32[2,1152]{1,0:T(2,128)S(1)}, f32[2,1152]{1,0:T(2,128)S(1)}, u32[]{:S(2)}, u32[]{:S(2)}) collective-permute-start(f32[2,1152]{1,0:T(2,128)S(1)} %copy.20), channel_id=1, source_target_pairs={{0,32},{32,64},{64,96},{96,128},{128,160},{160,192},{192,224},{224... | collective-permute-start | bytes 27656 | tf_op jit(solution)/shard_map/while/body/eval_jaxpr/ppermute | solution.py:12
  380.0 8.0 collective-permute-start.1
  388.0 11.1 %collective-permute-start = (f32[2,1152]{1,0:T(2,128)S(1)}, f32[2,1152]{1,0:T(2,128)S(1)}, u32[]{:S(2)}, u32[]{:S(2)}) collective-permute-start(f32[2,1152]{1,0:T(2,128)S(1)} %copy.20), channel_id=1, source_target_pairs={{0,32},{32,64},{64,96},{96,128},{128,160},{160,192},{192,224},{224... | collective-permute-start | bytes 27656 | tf_op jit(solution)/shard_map/while/body/eval_jaxpr/ppermute | solution.py:12
  391.1 8.0 collective-permute-start.1
  399.1 11.1 %collective-permute-start = (f32[2,1152]{1,0:T(2,128)S(1)}, f32[2,1152]{1,0:T(2,128)S(1)}, u32[]{:S(2)}, u32[]{:S(2)}) collective-permute-start(f32[2,1152]{1,0:T(2,128)S(1)} %copy.20), channel_id=1, source_target_pairs={{0,32},{32,64},{64,96},{96,128},{128,160},{160,192},{192,224},{224... | collective-permute-start | bytes 27656 | tf_op jit(solution)/shard_map/while/body/eval_jaxpr/ppermute | solution.py:12
  402.2 8.0 collective-permute-start.1
  410.2 2.4 copy-start.3
  417.2 1.2 copy-start.6
  421.2 288.2 %all-reduce.55.cloned.1.call-start = ((), (), s32[]{:S(2)}) async-start(), calls=%async_computation.6 | async-start | bytes 147456 | tf_op jit(solution)/shard_map/psum | solution.py:119
  559.3 428.8 %all-reduce.53.cloned.1.call-start = ((), (), s32[]{:S(2)}) async-start(), calls=%async_computation.4 | async-start | bytes 344064 | tf_op jit(solution)/shard_map/psum | solution.py:115
Sparse Core Ops, SparseCore 0:
  10.1 74.2 all-gather.3
  86.5 67.7 all-gather.5
  156.5 66.9 all-gather.7
  421.4 137.8 reduce-scatter.1
  562.0 147.3 all-reduce.54
  715.6 272.4 all-reduce.52
where the time goes:
time: 998 us; the launch traced here: 997 us
  waiting for transfers between devices  774 us (78%)
  starting transfers between devices  104 us (10%)
  other arithmetic  50 us (5%)
  matrix products  44.9 us (4%)
  between operations  15.4 us (2%)
    psum x1, waiting for transfers between devices, body(): kernel_grad = lax.psum(kernel_part, ('loop', 'dp'))  277 us
    psum x1, waiting for transfers between devices, body(): up_grad = lax.psum(up_rows, 'loop').astype(jnp.float32)  149 us
    reduce_scatter x1, waiting for transfers between devices, body(): lax.psum_scatter(up_part.astype(jnp.float32).astype(jnp.bfloat16), 'dp',...  119 us
    ppermute x32, starting transfers between devices, passed_along(): return lax.ppermute(value, axis, pairs)  104 us
    all_gather x1, waiting for transfers between devices, body(): lax.all_gather(w_down, 'dp', axis=0, tiled=True)  65.1 us
    all_gather x1, waiting for transfers between devices, body(): lax.all_gather(w_head, 'dp', axis=0, tiled=True)  64.5 us
    ppermute x32, waiting for transfers between devices, passed_along(): return lax.ppermute(value, axis, pairs)  59.5 us
    all_gather x1, waiting for transfers between devices, body(): lax.all_gather(w_up, 'dp', axis=0, tiled=True)  37.7 us
  transfers between devices with their start and end apart: 38, of which 22 were waited for; matrix products, arithmetic and copies ran while one was open for 9% of the time, Pallas kernels for 0%

commit v1 on v0

--- a/solution.py
+++ b/solution.py
@@ -112,7 +112,7 @@
         text_cot - text_hat * jnp.sum(text_hat * text_cot, axis=-1, keepdims=True)
     ) / text_norm
     kernel_part, up_part = pullback(image_cot)
-    kernel_grad = lax.psum(kernel_part, ("loop", "dp"))
+    kernel_grad = lax.psum(lax.psum(kernel_part, "loop"), "dp")
     up_rows = lax.psum_scatter(
         up_part.astype(jnp.float32).astype(jnp.bfloat16), "dp", scatter_dimension=0, tiled=True
     )

time: 998 us -> 1110 us (1.11)
  waiting for transfers between devices: 774 us -> 881 us
    psum x1 -> x2, waiting for transfers between devices: 277 us -> 379 us  [body(): kernel_grad = lax.psum(lax.psum(kernel_part, 'loop'), 'dp')]
  transfers between devices with their start and end apart: 38 -> 39, of which waited for: 22 -> 23; matrix products, arithmetic and copies ran while one was open for 9% -> 8% of each run, Pallas kernels for 0% -> 0%
where the time goes in v1:
time: 1110 us; the launch traced here: 1100 us
  waiting for transfers between devices  881 us (79%)
  starting transfers between devices  104 us (9%)
  other arithmetic  50.4 us (5%)
  matrix products  45 us (4%)
  between operations  15.4 us (1%)
    psum x2, waiting for transfers between devices, body(): kernel_grad = lax.psum(lax.psum(kernel_part, 'loop'), 'dp')  379 us
    psum x1, waiting for transfers between devices, body(): up_grad = lax.psum(up_rows, 'loop').astype(jnp.float32)  155 us
    reduce_scatter x1, waiting for transfers between devices, body(): lax.psum_scatter(up_part.astype(jnp.float32).astype(jnp.bfloat16), 'dp',...  119 us
    ppermute x32, starting transfers between devices, passed_along(): return lax.ppermute(value, axis, pairs)  104 us
    all_gather x1, waiting for transfers between devices, body(): lax.all_gather(w_down, 'dp', axis=0, tiled=True)  65.1 us
    all_gather x1, waiting for transfers between devices, body(): lax.all_gather(w_head, 'dp', axis=0, tiled=True)  64.5 us
    ppermute x32, waiting for transfers between devices, passed_along(): return lax.ppermute(value, axis, pairs)  59.3 us
    all_gather x1, waiting for transfers between devices, body(): lax.all_gather(w_up, 'dp', axis=0, tiled=True)  37.4 us
  transfers between devices with their start and end apart: 39, of which 23 were waited for; matrix products, arithmetic and copies ran while one was open for 8% of the time, Pallas kernels for 0%

profile of v1, /device:TPU:1, one launch (start us, length us, event | category | flops | bytes accessed | tf_op | source)
XLA Modules:
  0.0 1103.9 jit_solution(13268672736187167131)
XLA Ops:
  15.5 30.9 %fusion.140 = (f32[2,16,16]{2,1,0:T(8,128)S(1)}, f32[2,16,16,768]{3,2,1,0:T(8,128)S(1)}) fusion(f32[768]{0:T(1024)S(1)} %get-tuple-element.377, f32[768]{0:T(1024)S(1)} %get-tuple-element.378, f32[768]{0:T(1024)S(1)} %get-tuple-element.331, f32[768]{0:T(1024)S(1)} %get-tuple-element.332, f32[768]{0:T(1024)S(1)} %get-tuple-element.333, ...), kind=kLoop, calls=%fused_computation.374 | loop fusion | flops 57802240 | bytes 2511872 | tf_op jit(solution)/shard_map/jvp()/reduce_sum | solution.py:25
  47.0 37.4 %all-gather.4.cloned.1.call-done = bf16[768,1536]{1,0:T(8,128)(2,1)} async-done(((bf16[24,1536]{1,0:T(8,128)(2,1)}), bf16[768,1536]{1,0:T(8,128)(2,1)}) %all-gather.4.cloned.1.call-update) | async-done | bytes 2359312 | tf_op jit(solution)/shard_map/all_gather | solution.py:66
  84.4 4.8 convolution_add_fusion
  89.2 65.1 %all-gather.6.cloned.1.call-done = bf16[1536,768]{1,0:T(8,128)(2,1)} async-done(((bf16[48,768]{1,0:T(8,128)(2,1)}), bf16[1536,768]{1,0:T(8,128)(2,1)}) %all-gather.6.cloned.1.call-update) | async-done | bytes 2359312 | tf_op jit(solution)/shard_map/all_gather | solution.py:67
  154.3 4.6 bitcast_reduce_fusion
  158.9 64.5 %all-gather.8.cloned.1.call-done = bf16[768,1152]{1,0:T(8,128)(2,1)} async-done(((bf16[24,1152]{1,0:T(8,128)(2,1)}), bf16[768,1152]{1,0:T(8,128)(2,1)}) %all-gather.8.cloned.1.call-update) | async-done | bytes 1769488 | tf_op jit(solution)/shard_map/all_gather | solution.py:68
  225.5 184.7 %while.20 = (s32[]{:T(128)}, f32[2,1152]{1,0:T(2,128)S(1)}, f32[2,1152]{1,0:T(2,128)S(1)}, f32[2,1152]{1,0:T(2,128)S(1)}, f32[]{:T(128)}, /*index=5*/s32[1,2]{1,...) while((s32[]{:T(128)}, f32[2,1152]{1,0:T(2,128)S(1)}, ...), condition=%wide.region_6.7_spmd.clone, body=%wide.region_5.6_spmd.clone.sunk | while | flops 177470 | bytes 166336 | solution.py:110
  225.5 4.3 collective-permute-start
  231.0 3.4 collective-permute-start.1
  234.6 4.4 collective-permute-done.1
  242.1 4.6 collective-permute-start.1
  246.8 3.2 collective-permute-done.1
  253.7 3.4 collective-permute-start.1
  257.3 4.4 collective-permute-done.1
  264.8 4.6 collective-permute-start.1
  269.6 3.2 collective-permute-done.1
  276.4 3.4 collective-permute-start.1
  280.0 4.4 collective-permute-done.1
  287.5 4.6 collective-permute-start.1
  292.3 3.2 collective-permute-done.1
  299.1 5.2 collective-permute-start.1
  311.4 6.0 collective-permute-start.1
  319.4 3.9 collective-permute-start
  324.5 3.9 collective-permute-start.1
  328.5 4.0 collective-permute-done.1
  335.6 3.8 collective-permute-start.1
  339.6 4.0 collective-permute-done.1
  346.7 3.8 collective-permute-start.1
  350.7 4.1 collective-permute-done.1
  357.8 3.8 collective-permute-start.1
  361.8 4.1 collective-permute-done.1
  368.9 3.8 collective-permute-start.1
  372.9 4.0 collective-permute-done.1
  380.0 3.8 collective-permute-start.1
  384.0 4.0 collective-permute-done.1
  391.1 3.8 collective-permute-start.1
  395.1 4.0 collective-permute-done.1
  402.2 4.1 collective-permute-start.1
  406.5 3.7 collective-permute-done.1
  412.6 4.6 fusion.14
  421.3 3.6 fusion.143
  426.0 5.0 fusion.117
  431.2 3.7 fusion.23
  434.9 3.9 fusion.118
  440.2 119.0 %reduce-scatter.2.cloned.1.call-done = bf16[24,1536]{1,0:T(8,128)(2,1)} async-done(((bf16[768,1536]{1,0:T(8,128)(2,1)}), bf16[24,1536]{1,0:T(8,128)(2,1)}) %reduce-scatter.2.cloned.1.call-update) | async-done | bytes 73744 | tf_op jit(solution)/shard_map/reduce_scatter | solution.py:116
  559.4 154.8 %all-reduce.54.cloned.1.call-done = f32[7,7,768]{2,1,0:T(8,128)} async-done(((f32[7,7,768]{2,1,0:T(8,128)}), f32[7,7,768]{2,1,0:T(8,128)}) %all-reduce.54.cloned.1.call-update) | async-done | bytes 150544 | tf_op jit(solution)/shard_map/psum | solution.py:115
  715.0 155.0 %all-reduce.58.cloned.1.call-done = bf16[24,1536]{1,0:T(8,128)(2,1)} async-done(((bf16[24,1536]{1,0:T(8,128)(2,1)}), bf16[24,1536]{1,0:T(8,128)(2,1)}) %all-reduce.58.cloned.1.call-update) | async-done | bytes 73744 | tf_op jit(solution)/shard_map/psum | solution.py:119
  871.6 223.9 %all-reduce.56.cloned.1.call-done = f32[7,7,768]{2,1,0:T(8,128)} async-done(((f32[7,7,768]{2,1,0:T(8,128)}), f32[7,7,768]{2,1,0:T(8,128)}) %all-reduce.56.cloned.1.call-update) | async-done | bytes 150544 | tf_op jit(solution)/shard_map/psum | solution.py:115
  (219 shorter events, 77.6 us)
Async XLA Ops:
  7.2 77.2 %all-gather.4.cloned.1.call-start = ((), (), s32[]{:S(2)}) async-start(), calls=%async_computation.1 | async-start | bytes 2433024 | tf_op jit(solution)/shard_map/all_gather | solution.py:66
  7.9 146.4 %all-gather.6.cloned.1.call-start = ((), (), s32[]{:S(2)}) async-start(), calls=%async_computation.2 | async-start | bytes 2433024 | tf_op jit(solution)/shard_map/all_gather | solution.py:67
  8.6 214.8 %all-gather.8.cloned.1.call-start = ((), (), s32[]{:S(2)}) async-start(), calls=%async_computation.3 | async-start | bytes 1824768 | tf_op jit(solution)/shard_map/all_gather | solution.py:68
  9.4 549.9 %reduce-scatter.2.cloned.1.call-start = ((), (), s32[]{:S(2)}) async-start(), calls=%async_computation.6 | async-start | bytes 2433024 | tf_op jit(solution)/shard_map/reduce_scatter | solution.py:116
  15.5 31.2 %copy-start.1 = (f32[768]{0:T(1024)S(1)}, f32[768]{0:T(1024)}, u32[]{:S(2)}) copy-start(f32[768]{0:T(1024)} %param.16) | copy-start | bytes 9220
  46.7 37.7 %copy-start.4 = (f32[1536]{0:T(1024)S(1)}, f32[1536]{0:T(1024)}, u32[]{:S(2)}) copy-start(f32[1536]{0:T(1024)} %param.18) | copy-start | bytes 18436
  84.4 69.9 %copy-start = (bf16[1,2,16,16,768]{4,3,2,1,0:T(8,128)(2,1)S(1)}, bf16[1,2,16,16,768]{4,3,2,1,0:T(8,128)(2,1)}, u32[]{:S(2)}) copy-start(bf16[1,2,16,16,768]{4,3,2,1,0:T(8,128)(2,1)} %param.14) | copy-start | bytes 2359300
  84.4 69.9 %copy-start.2 = (f32[768]{0:T(1024)S(1)}, f32[768]{0:T(1024)}, u32[]{:S(2)}) copy-start(f32[768]{0:T(1024)} %param.20) | copy-start | bytes 9220
  158.9 66.5 %copy-start.5 = (s32[1,2]{1,0:T(1,128)S(1)}, s32[1,2]{1,0:T(1,128)}, u32[]{:S(2)}) copy-start(s32[1,2]{1,0:T(1,128)} %param.23) | copy-start | bytes 28
  225.5 13.5 %collective-permute-start = (f32[2,1152]{1,0:T(2,128)S(1)}, f32[2,1152]{1,0:T(2,128)S(1)}, u32[]{:S(2)}, u32[]{:S(2)}) collective-permute-start(f32[2,1152]{1,0:T(2,128)S(1)} %copy.20), channel_id=1, source_target_pairs={{0,32},{32,64},{64,96},{96,128},{128,160},{160,192},{192,224},{224... | collective-permute-start | bytes 27656 | tf_op jit(solution)/shard_map/while/body/eval_jaxpr/ppermute | solution.py:12
  231.0 8.0 collective-permute-start.1
  239.0 11.1 %collective-permute-start = (f32[2,1152]{1,0:T(2,128)S(1)}, f32[2,1152]{1,0:T(2,128)S(1)}, u32[]{:S(2)}, u32[]{:S(2)}) collective-permute-start(f32[2,1152]{1,0:T(2,128)S(1)} %copy.20), channel_id=1, source_target_pairs={{0,32},{32,64},{64,96},{96,128},{128,160},{160,192},{192,224},{224... | collective-permute-start | bytes 27656 | tf_op jit(solution)/shard_map/while/body/eval_jaxpr/ppermute | solution.py:12
  242.1 8.0 collective-permute-start.1
  250.1 11.6 %collective-permute-start = (f32[2,1152]{1,0:T(2,128)S(1)}, f32[2,1152]{1,0:T(2,128)S(1)}, u32[]{:S(2)}, u32[]{:S(2)}) collective-permute-start(f32[2,1152]{1,0:T(2,128)S(1)} %copy.20), channel_id=1, source_target_pairs={{0,32},{32,64},{64,96},{96,128},{128,160},{160,192},{192,224},{224... | collective-permute-start | bytes 27656 | tf_op jit(solution)/shard_map/while/body/eval_jaxpr/ppermute | solution.py:12
  253.7 8.0 collective-permute-start.1
  261.7 11.1 %collective-permute-start = (f32[2,1152]{1,0:T(2,128)S(1)}, f32[2,1152]{1,0:T(2,128)S(1)}, u32[]{:S(2)}, u32[]{:S(2)}) collective-permute-start(f32[2,1152]{1,0:T(2,128)S(1)} %copy.20), channel_id=1, source_target_pairs={{0,32},{32,64},{64,96},{96,128},{128,160},{160,192},{192,224},{224... | collective-permute-start | bytes 27656 | tf_op jit(solution)/shard_map/while/body/eval_jaxpr/ppermute | solution.py:12
  264.8 8.0 collective-permute-start.1
  272.8 11.6 %collective-permute-start = (f32[2,1152]{1,0:T(2,128)S(1)}, f32[2,1152]{1,0:T(2,128)S(1)}, u32[]{:S(2)}, u32[]{:S(2)}) collective-permute-start(f32[2,1152]{1,0:T(2,128)S(1)} %copy.20), channel_id=1, source_target_pairs={{0,32},{32,64},{64,96},{96,128},{128,160},{160,192},{192,224},{224... | collective-permute-start | bytes 27656 | tf_op jit(solution)/shard_map/while/body/eval_jaxpr/ppermute | solution.py:12
  276.4 8.0 collective-permute-start.1
  284.4 11.1 %collective-permute-start = (f32[2,1152]{1,0:T(2,128)S(1)}, f32[2,1152]{1,0:T(2,128)S(1)}, u32[]{:S(2)}, u32[]{:S(2)}) collective-permute-start(f32[2,1152]{1,0:T(2,128)S(1)} %copy.20), channel_id=1, source_target_pairs={{0,32},{32,64},{64,96},{96,128},{128,160},{160,192},{192,224},{224... | collective-permute-start | bytes 27656 | tf_op jit(solution)/shard_map/while/body/eval_jaxpr/ppermute | solution.py:12
  287.5 8.0 collective-permute-start.1
  295.5 11.6 %collective-permute-start = (f32[2,1152]{1,0:T(2,128)S(1)}, f32[2,1152]{1,0:T(2,128)S(1)}, u32[]{:S(2)}, u32[]{:S(2)}) collective-permute-start(f32[2,1152]{1,0:T(2,128)S(1)} %copy.20), channel_id=1, source_target_pairs={{0,32},{32,64},{64,96},{96,128},{128,160},{160,192},{192,224},{224... | collective-permute-start | bytes 27656 | tf_op jit(solution)/shard_map/while/body/eval_jaxpr/ppermute | solution.py:12
  299.1 8.0 collective-permute-start.1
  307.2 12.2 %collective-permute-start = (f32[2,1152]{1,0:T(2,128)S(1)}, f32[2,1152]{1,0:T(2,128)S(1)}, u32[]{:S(2)}, u32[]{:S(2)}) collective-permute-start(f32[2,1152]{1,0:T(2,128)S(1)} %copy.20), channel_id=1, source_target_pairs={{0,32},{32,64},{64,96},{96,128},{128,160},{160,192},{192,224},{224... | collective-permute-start | bytes 27656 | tf_op jit(solution)/shard_map/while/body/eval_jaxpr/ppermute | solution.py:12
  311.4 8.0 collective-permute-start.1
  319.4 13.1 %collective-permute-start = (f32[2,1152]{1,0:T(2,128)S(1)}, f32[2,1152]{1,0:T(2,128)S(1)}, u32[]{:S(2)}, u32[]{:S(2)}) collective-permute-start(f32[2,1152]{1,0:T(2,128)S(1)} %copy.20), channel_id=1, source_target_pairs={{0,32},{32,64},{64,96},{96,128},{128,160},{160,192},{192,224},{224... | collective-permute-start | bytes 27656 | tf_op jit(solution)/shard_map/while/body/eval_jaxpr/ppermute | solution.py:12
  324.5 8.0 collective-permute-start.1
  332.5 11.2 %collective-permute-start = (f32[2,1152]{1,0:T(2,128)S(1)}, f32[2,1152]{1,0:T(2,128)S(1)}, u32[]{:S(2)}, u32[]{:S(2)}) collective-permute-start(f32[2,1152]{1,0:T(2,128)S(1)} %copy.20), channel_id=1, source_target_pairs={{0,32},{32,64},{64,96},{96,128},{128,160},{160,192},{192,224},{224... | collective-permute-start | bytes 27656 | tf_op jit(solution)/shard_map/while/body/eval_jaxpr/ppermute | solution.py:12
  335.6 8.0 collective-permute-start.1
  343.7 11.1 %collective-permute-start = (f32[2,1152]{1,0:T(2,128)S(1)}, f32[2,1152]{1,0:T(2,128)S(1)}, u32[]{:S(2)}, u32[]{:S(2)}) collective-permute-start(f32[2,1152]{1,0:T(2,128)S(1)} %copy.20), channel_id=1, source_target_pairs={{0,32},{32,64},{64,96},{96,128},{128,160},{160,192},{192,224},{224... | collective-permute-start | bytes 27656 | tf_op jit(solution)/shard_map/while/body/eval_jaxpr/ppermute | solution.py:12
  346.7 8.0 collective-permute-start.1
  354.8 11.1 %collective-permute-start = (f32[2,1152]{1,0:T(2,128)S(1)}, f32[2,1152]{1,0:T(2,128)S(1)}, u32[]{:S(2)}, u32[]{:S(2)}) collective-permute-start(f32[2,1152]{1,0:T(2,128)S(1)} %copy.20), channel_id=1, source_target_pairs={{0,32},{32,64},{64,96},{96,128},{128,160},{160,192},{192,224},{224... | collective-permute-start | bytes 27656 | tf_op jit(solution)/shard_map/while/body/eval_jaxpr/ppermute | solution.py:12
  357.8 8.0 collective-permute-start.1
  365.8 11.1 %collective-permute-start = (f32[2,1152]{1,0:T(2,128)S(1)}, f32[2,1152]{1,0:T(2,128)S(1)}, u32[]{:S(2)}, u32[]{:S(2)}) collective-permute-start(f32[2,1152]{1,0:T(2,128)S(1)} %copy.20), channel_id=1, source_target_pairs={{0,32},{32,64},{64,96},{96,128},{128,160},{160,192},{192,224},{224... | collective-permute-start | bytes 27656 | tf_op jit(solution)/shard_map/while/body/eval_jaxpr/ppermute | solution.py:12
  368.9 8.0 collective-permute-start.1
  376.9 11.1 %collective-permute-start = (f32[2,1152]{1,0:T(2,128)S(1)}, f32[2,1152]{1,0:T(2,128)S(1)}, u32[]{:S(2)}, u32[]{:S(2)}) collective-permute-start(f32[2,1152]{1,0:T(2,128)S(1)} %copy.20), channel_id=1, source_target_pairs={{0,32},{32,64},{64,96},{96,128},{128,160},{160,192},{192,224},{224... | collective-permute-start | bytes 27656 | tf_op jit(solution)/shard_map/while/body/eval_jaxpr/ppermute | solution.py:12
  380.0 8.0 collective-permute-start.1
  388.0 11.1 %collective-permute-start = (f32[2,1152]{1,0:T(2,128)S(1)}, f32[2,1152]{1,0:T(2,128)S(1)}, u32[]{:S(2)}, u32[]{:S(2)}) collective-permute-start(f32[2,1152]{1,0:T(2,128)S(1)} %copy.20), channel_id=1, source_target_pairs={{0,32},{32,64},{64,96},{96,128},{128,160},{160,192},{192,224},{224... | collective-permute-start | bytes 27656 | tf_op jit(solution)/shard_map/while/body/eval_jaxpr/ppermute | solution.py:12
  391.1 8.0 collective-permute-start.1
  399.1 11.1 %collective-permute-start = (f32[2,1152]{1,0:T(2,128)S(1)}, f32[2,1152]{1,0:T(2,128)S(1)}, u32[]{:S(2)}, u32[]{:S(2)}) collective-permute-start(f32[2,1152]{1,0:T(2,128)S(1)} %copy.20), channel_id=1, source_target_pairs={{0,32},{32,64},{64,96},{96,128},{128,160},{160,192},{192,224},{224... | collective-permute-start | bytes 27656 | tf_op jit(solution)/shard_map/while/body/eval_jaxpr/ppermute | solution.py:12
  402.2 8.0 collective-permute-start.1
  410.2 2.4 copy-start.3
  417.2 1.2 copy-start.6
  421.3 293.0 %all-reduce.54.cloned.1.call-start = ((), (), s32[]{:S(2)}) async-start(), calls=%async_computation.4 | async-start | bytes 344064 | tf_op jit(solution)/shard_map/psum | solution.py:115
  440.2 429.8 %all-reduce.58.cloned.1.call-start = ((), (), s32[]{:S(2)}) async-start(), calls=%async_computation.7 | async-start | bytes 147456 | tf_op jit(solution)/shard_map/psum | solution.py:119
  559.3 536.2 %all-reduce.56.cloned.1.call-start = ((), (), s32[]{:S(2)}) async-start(), calls=%async_computation.5 | async-start | bytes 344064 | tf_op jit(solution)/shard_map/psum | solution.py:115
Sparse Core Ops, SparseCore 0:
  10.1 74.2 all-gather.3
  86.5 67.7 all-gather.5
  156.5 66.9 all-gather.7
  421.4 137.7 reduce-scatter.1
  562.6 151.6 all-reduce.53
  717.3 152.6 all-reduce.57
  872.9 222.4 all-reduce.55
